TPU v7x, 32 devices: a whole 2x2x4 slice. The times are simulated.
32 devices in a mesh: link: 16 (over z, x, core), col: 2 (over y).
Axes of the slice: x: 2, y: 2, z: 4, core: 2. Of those that a mesh axis runs over, the one named last changes fastest.
Arguments:
- values: bfloat16 [256, 16, 128], P('link'), may hold values from -6 to 6
- tiles: int32 [256, 16], P('link'), may hold values from 0 to 31, all different within a row
- barrier: float32 [256], P('link'), may hold values from 0.5 to 2
- slack: float32 [4096], replicated, may hold values from 0.5 to 2
- order: int32 [32], replicated, may hold values from 0 to 31, each once
Outputs:
- factored: float32 [4096, 4096], P('link', 'col')
Inputs may be any that keep to these rules, and one draw needn't show every extreme that they name: `tiles`: each commodity's 16 tile numbers are distinct, and every tile is named by some commodity. `order`: each tile number appears once.
All inputs are finite; a program needn't handle non-finite values.
Results may differ from a plain program's by a relative error of at most 0.0038.
Values may be sent and summed in bfloat16 or wider, within the bound.
A program may use at most 64 MiB of HBM per device.

v0:
```python
import jax
import jax.numpy as jnp
from jax import lax
from jax.sharding import PartitionSpec as P

PANEL = 128


def spread_2(value, axis, source):
    kept = jnp.where(lax.axis_index(axis) == source, value, 0).astype(value.dtype)
    return lax.psum(kept, axis)


def densify(tile_vals, tile_ids, targets):
    onehot = (tile_ids[:, :, None] == targets[None, None, :]).astype(jnp.bfloat16)
    dense_out = jnp.einsum("kjp,kju->kpu", onehot, tile_vals, preferred_element_type=jnp.float32)
    dense_out = dense_out.astype(jnp.bfloat16)
    return dense_out.reshape(tile_vals.shape[0], targets.shape[0] * tile_vals.shape[2])


def contract_rows(left_side, right_side):
    return lax.dot_general(
        left_side, right_side, (((0,), (0,)), ((), ())), preferred_element_type=jnp.float32
    )


def local(values, tiles, barrier, slack, order):
    link_devs = lax.axis_size("link")
    col_devs = lax.axis_size("col")
    link_idx = lax.axis_index("link")
    col_idx = lax.axis_index("col")
    link_count = slack.shape[0]
    rows_dev = link_count // link_devs
    cols_dev = link_count // col_devs
    tile_len = values.shape[2]
    ntiles = order.shape[0]
    factor = link_count / (values.shape[0] * link_devs * values.shape[1] * tile_len)
    scaled = (jnp.sqrt(barrier * factor)[:, None, None] * values.astype(jnp.float32)).astype(
        jnp.bfloat16
    )
    own_dense = densify(scaled, tiles, order)
    link_rows = lax.all_to_all(own_dense, "link", split_axis=1, concat_axis=0, tiled=True)
    col_slab = lax.dynamic_slice_in_dim(own_dense, col_idx * cols_dev, cols_dev, 1)
    normal = contract_rows(link_rows, lax.all_gather(col_slab, "link", axis=0, tiled=True))
    rows_g = link_idx * rows_dev + jnp.arange(rows_dev)
    cols_g = col_idx * cols_dev + jnp.arange(cols_dev)
    perm_hot = (order[:, None] == jnp.arange(ntiles)[None, :]).astype(jnp.float32)
    slack_ord = jnp.dot(
        perm_hot, slack.reshape(ntiles, tile_len), precision=lax.Precision.HIGHEST
    ).reshape(link_count)
    slack_rows = lax.dynamic_slice_in_dim(slack_ord, link_idx * rows_dev, rows_dev)
    matrix = normal + jnp.where(
        rows_g[:, None] == cols_g[None, :], slack_rows[:, None], jnp.float32(0.0)
    )
    panels = []
    for panel_no in range(2):
        first_col = panel_no * PANEL
        diag_block = matrix[first_col : first_col + PANEL, first_col : first_col + PANEL]
        factor_local = jnp.linalg.cholesky(diag_block)
        lower_fac = spread_2(factor_local, "col", 0)
        solved = jax.scipy.linalg.solve_triangular(
            lower_fac, matrix[first_col : first_col + PANEL, :], lower=True
        )
        picker = (jnp.arange(PANEL)[:, None] == (cols_g - first_col)[None, :]).astype(jnp.float32)
        diag_cols = jnp.dot(lower_fac.T, picker, precision=lax.Precision.HIGHEST)
        row_form = jnp.where(
            cols_g[None, :] < first_col,
            jnp.float32(0.0),
            jnp.where(cols_g[None, :] < first_col + PANEL, diag_cols, solved),
        )
        spread = spread_2(row_form, "link", 0)
        owner_col = link_idx * rows_dev // cols_dev
        offset = link_idx * rows_dev - owner_col * cols_dev
        my_rows = lax.dynamic_slice_in_dim(spread, offset, rows_dev, 1).T
        column = spread_2(my_rows, "col", owner_col)
        matrix = matrix - jnp.dot(
            column.astype(jnp.bfloat16),
            spread.astype(jnp.bfloat16),
            preferred_element_type=jnp.float32,
        )
        panels.append(column)
    panel_block = jnp.concatenate(panels, 1)
    padded = jnp.pad(panel_block, ((0, 0), (0, cols_dev - 2 * PANEL)))
    return jnp.where(
        cols_g[None, :] < 2 * PANEL,
        padded,
        jnp.where(rows_g[:, None] < 2 * PANEL, jnp.float32(0.0), matrix),
    )


def solution(mesh):
    in_specs = (P("link", None, None), P("link", None), P("link"), P(), P())
    out_specs = P("link", "col")
    return jax.shard_map(local, mesh=mesh, in_specs=in_specs, out_specs=out_specs, check_vma=False)
```

profile of v0, /device:TPU:11, one launch (start us, length us, event | category | flops | bytes accessed | tf_op | source)
XLA Modules:
  0.0 398.2 jit_solution(1611759713158489388)
XLA Ops:
  9.9 6.6 %all-to-all-start = ((bf16[16,16,256]{2,0,1:T(8,128)(2,1)}), bf16[16,16,256]{2,0,1:T(8,128)(2,1)S(1)}, u32[]{:S(2)}, u32[]{:S(2)}) async-start(bf16[16,16,256]{2,0,1:T(8,128)(2,1)} %copy.12), calls=%async_computation | async-start | bytes 262144 | tf_op jit(solution)/shard_map/all_to_all | solution.py:42
  17.4 4.2 %all-to-all-done = bf16[16,16,256]{2,0,1:T(8,128)(2,1)S(1)} async-done(((bf16[16,16,256]{2,0,1:T(8,128)(2,1)}), bf16[16,16,256]{2,0,1:T(8,128)(2,1)S(1)}, u32[]{:S(2)}, u32[]{:S(2)}) %all-to-all-start) | async-done | bytes 131104 | tf_op jit(solution)/shard_map/all_to_all | solution.py:42
  21.6 26.3 %all-gather.2.cloned.1.call-done = bf16[256,2048]{1,0:T(8,128)(2,1)} async-done(((bf16[16,2048]{1,0:T(8,128)(2,1)}), bf16[256,2048]{1,0:T(8,128)(2,1)}) %all-gather.2.cloned.1.call-update) | async-done | bytes 1048592 | tf_op jit(solution)/shard_map/all_gather | solution.py:44
  47.9 1.9 convolution_add_fusion
  50.0 11.7 %cholesky.44 = f32[128,128]{1,0:T(8,128)S(1)} custom-call(f32[128,128]{1,0:T(8,128)S(1)} %fusion.18), custom_call_target="Cholesky" | custom-call | tf_op jit(solution)/shard_map/jit(cholesky)/cholesky | solution.py:59
  62.5 1.3 select_select_fusion.1
  63.9 20.2 %all-reduce.8.cloned.1.call-done = f32[128,128]{1,0:T(8,128)} async-done(((f32[128,128]{1,0:T(8,128)}), f32[128,128]{1,0:T(8,128)}) %all-reduce.8.cloned.1.call-update) | async-done | bytes 65552 | tf_op jit(solution)/shard_map/psum | solution.py:11
  84.9 9.8 %custom-call.6 = f32[1,128,128]{1,2,0:T(8,128)S(1)} custom-call(f32[1,128,128]{2,1,0:T(8,128)S(1)} %select_bitcast_fusion.3), custom_call_target="InvertDiagBlocksLowerTriangular" | custom-call | tf_op jit(solution)/shard_map/jit(_solve_triangular)/triangular_solve | solution.py:61
  94.7 1.5 fusion.8
  96.2 2.1 fusion.5
  98.4 91.8 %all-reduce.10.cloned.1.call-done = f32[128,2048]{1,0:T(8,128)} async-done(((f32[128,2048]{1,0:T(8,128)}), f32[128,2048]{1,0:T(8,128)}) %all-reduce.10.cloned.1.call-update) | async-done | bytes 1048592 | tf_op jit(solution)/shard_map/psum | solution.py:11
  190.2 1.6 select_bitcast_fusion.1
  192.0 22.6 %all-reduce.12.cloned.1.call-done = f32[256,128]{0,1:T(8,128)} async-done(((f32[256,128]{0,1:T(8,128)}), f32[256,128]{0,1:T(8,128)}) %all-reduce.12.cloned.1.call-update) | async-done | bytes 131088 | tf_op jit(solution)/shard_map/psum | solution.py:11
  214.6 1.8 convolution_subtract_fusion.1
  218.7 11.7 %cholesky.55 = f32[128,128]{1,0:T(8,128)S(1)} custom-call(f32[128,128]{1,0:T(8,128)S(1)} %fusion.16), custom_call_target="Cholesky" | custom-call | tf_op jit(solution)/shard_map/jit(cholesky)/cholesky | solution.py:59
  232.4 20.9 %all-reduce.14.cloned.1.call-done = f32[128,128]{1,0:T(8,128)} async-done(((f32[128,128]{1,0:T(8,128)}), f32[128,128]{1,0:T(8,128)}) %all-reduce.14.cloned.1.call-update) | async-done | bytes 65552 | tf_op jit(solution)/shard_map/psum | solution.py:11
  254.2 9.8 %custom-call.7 = f32[1,128,128]{1,2,0:T(8,128)S(1)} custom-call(f32[1,128,128]{2,1,0:T(8,128)S(1)} %select_bitcast_fusion.2), custom_call_target="InvertDiagBlocksLowerTriangular" | custom-call | tf_op jit(solution)/shard_map/jit(_solve_triangular)/triangular_solve | solution.py:61
  264.0 1.5 fusion.9
  265.5 3.5 fusion.3
  269.0 91.6 %all-reduce.16.cloned.1.call-done = f32[128,2048]{1,0:T(8,128)} async-done(((f32[128,2048]{1,0:T(8,128)}), f32[128,2048]{1,0:T(8,128)}) %all-reduce.16.cloned.1.call-update) | async-done | bytes 1048592 | tf_op jit(solution)/shard_map/psum | solution.py:11
  360.6 1.6 select_bitcast_fusion
  362.2 23.0 %all-reduce.18.cloned.1.call-done = f32[256,128]{0,1:T(8,128)} async-done(((f32[256,128]{0,1:T(8,128)}), f32[256,128]{0,1:T(8,128)}) %all-reduce.18.cloned.1.call-update) | async-done | bytes 131088 | tf_op jit(solution)/shard_map/psum | solution.py:11
  385.2 3.2 fusion.1
  388.4 2.9 copy.18
  (49 shorter events, 11.6 us)
Async XLA Ops:
  6.5 10.0 %copy-start = (f32[4096]{0:T(1024)S(1)}, f32[4096]{0:T(1024)}, u32[]{:S(2)}) copy-start(f32[4096]{0:T(1024)} %param.11) | copy-start | bytes 49156
  6.5 41.4 %all-gather.2.cloned.1.call-start = ((), (), s32[]{:S(2)}) async-start(), calls=%async_computation.1 | async-start | bytes 1114112 | tf_op jit(solution)/shard_map/all_gather | solution.py:44
  9.9 11.7 %all-to-all-start = ((bf16[16,16,256]{2,0,1:T(8,128)(2,1)}), bf16[16,16,256]{2,0,1:T(8,128)(2,1)S(1)}, u32[]{:S(2)}, u32[]{:S(2)}) async-start(bf16[16,16,256]{2,0,1:T(8,128)(2,1)} %copy.12), calls=%async_computation | async-start | bytes 262144 | tf_op jit(solution)/shard_map/all_to_all | solution.py:42
  16.5 67.6 %all-reduce.8.cloned.1.call-start = ((), (), s32[]{:S(2)}) async-start(), calls=%async_computation.2 | async-start | bytes 131072 | tf_op jit(solution)/shard_map/psum | solution.py:11
  63.8 126.4 %all-reduce.10.cloned.1.call-start = ((), (), s32[]{:S(2)}) async-start(), calls=%async_computation.3 | async-start | bytes 2097152 | tf_op jit(solution)/shard_map/psum | solution.py:11
  98.3 116.3 %all-reduce.12.cloned.1.call-start = ((), (), s32[]{:S(2)}) async-start(), calls=%async_computation.4 | async-start | bytes 262144 | tf_op jit(solution)/shard_map/psum | solution.py:11
  191.8 61.5 %all-reduce.14.cloned.1.call-start = ((), (), s32[]{:S(2)}) async-start(), calls=%async_computation.5 | async-start | bytes 131072 | tf_op jit(solution)/shard_map/psum | solution.py:11
  216.4 1.3 copy-start.1
  232.3 128.3 %all-reduce.16.cloned.1.call-start = ((), (), s32[]{:S(2)}) async-start(), calls=%async_computation.6 | async-start | bytes 2097152 | tf_op jit(solution)/shard_map/psum | solution.py:11
  265.4 119.8 %copy-start.2 = (f32[256,2048]{0,1:T(8,128)S(1)}, f32[256,2048]{0,1:T(8,128)}, u32[]{:S(2)}) copy-start(f32[256,2048]{0,1:T(8,128)} %copy-done.1) | copy-start | bytes 6291460
  265.5 119.8 %copy-start.3 = (f32[256,128]{0,1:T(8,128)S(1)}, f32[256,128]{0,1:T(8,128)}, u32[]{:S(2)}) copy-start(f32[256,128]{0,1:T(8,128)} %all-reduce.12.cloned.1.call-done) | copy-start | bytes 393220
  269.0 116.2 %all-reduce.18.cloned.1.call-start = ((), (), s32[]{:S(2)}) async-start(), calls=%async_computation.7 | async-start | bytes 262144 | tf_op jit(solution)/shard_map/psum | solution.py:11
Sparse Core Ops, SparseCore 0:
  9.5 38.3 all-gather.1
  63.9 20.0 all-reduce.7
  98.4 91.7 all-reduce.9
  192.3 22.2 all-reduce.11
  232.5 20.7 all-reduce.13
  269.1 91.5 all-reduce.15
  362.9 22.2 all-reduce.17
where the time goes:
time: 401 us; the launch traced here: 398 us
  waiting for transfers between devices  301 us (75%)
  other arithmetic  53.5 us (13%)
  matrix products  17.5 us (4%)
  between operations  13.7 us (3%)
  starting transfers between devices  6.98 us (2%)
  local copies, waits for them, and re-layouts  5.92 us (1%)
    psum x6, waiting for transfers between devices, spread_2(): return lax.psum(kept, axis)  270 us
    all_gather x1, waiting for transfers between devices, local(): lax.all_gather(col_slab, 'link', axis=0, tiled=True)  26.3 us
    another operation x6, other arithmetic, local(): factor_local = jnp.linalg.cholesky(diag_block)  24.9 us
    another operation x4, other arithmetic, local(): jax.scipy.linalg.solve_triangular(lower_fac, matrix[first_col:first_col +...  21.3 us
  transfers between devices with their start and end apart: 8, of which 8 were waited for; matrix products, arithmetic and copies ran while one was open for 0% of the time, Pallas kernels for 0%

commit v1 on v0

v1 whole, which is shorter than its diff:
```python
import jax
import jax.numpy as jnp
from jax import lax
from jax.sharding import PartitionSpec as P

PANEL = 128


def contract_rows(left_side, right_side):
    return lax.dot_general(
        left_side, right_side, (((0,), (0,)), ((), ())), preferred_element_type=jnp.float32
    )


def local(values, tiles, barrier, slack, order):
    link_devs = lax.axis_size("link")
    col_devs = lax.axis_size("col")
    link_idx = lax.axis_index("link")
    col_idx = lax.axis_index("col")
    link_count = slack.shape[0]
    rows_dev = link_count // link_devs
    cols_dev = link_count // col_devs
    tpc, tile_len = values.shape[1:]
    ntiles = order.shape[0]
    head = 2 * PANEL
    factor = link_count / (values.shape[0] * link_devs * tpc * tile_len)
    scaled = (jnp.sqrt(barrier * factor)[:, None, None] * values.astype(jnp.float32)).astype(
        jnp.bfloat16
    )
    ids = jnp.pad(tiles.astype(jnp.bfloat16), ((0, 0), (0, tile_len - tpc)))
    packed = jnp.concatenate([scaled, ids[:, None, :]], 1)
    packed = lax.all_gather(packed, "link", axis=0, tiled=True)
    all_vals = packed[:, :tpc]
    all_ids = packed[:, tpc, :tpc].astype(jnp.int32)

    row_tiles = rows_dev // tile_len
    col_tiles = cols_dev // tile_len
    places = jnp.concatenate(
        [
            jnp.arange(head // tile_len),
            link_idx * row_tiles + jnp.arange(row_tiles),
            col_idx * col_tiles + jnp.arange(col_tiles),
        ]
    )
    place_hot = (places[:, None] == jnp.arange(ntiles)[None, :]).astype(jnp.int32)
    targets = jnp.sum(place_hot * order[None, :], 1)
    onehot = (all_ids[:, :, None] == targets[None, None, :]).astype(jnp.bfloat16)
    chosen = jnp.einsum("kjp,kju->kpu", onehot, all_vals, preferred_element_type=jnp.float32)
    chosen = chosen.astype(jnp.bfloat16).reshape(all_vals.shape[0], -1)
    cols_g = (places[:, None] * tile_len + jnp.arange(tile_len)[None, :]).reshape(-1)

    target_hot = (targets[: head // tile_len + row_tiles, None] == jnp.arange(ntiles)).astype(
        jnp.float32
    )
    slack_some = jnp.dot(
        target_hot, slack.reshape(ntiles, tile_len), precision=lax.Precision.HIGHEST
    ).reshape(-1)
    slack_head, slack_rows = slack_some[:head], slack_some[head:]

    panel_rows = jnp.arange(head)
    strip = contract_rows(chosen[:, :head], chosen)
    strip = strip + jnp.where(
        panel_rows[:, None] == cols_g[None, :], slack_head[:, None], jnp.float32(0.0)
    )
    keep = panel_rows[:, None] <= cols_g[None, :]
    done = []
    work = strip[:PANEL]
    for panel_no in range(2):
        first = panel_no * PANEL
        lower_fac = jnp.linalg.cholesky(work[:, first : first + PANEL])
        solved = jax.scipy.linalg.solve_triangular(lower_fac, work, lower=True)
        solved = jnp.where(keep[first : first + PANEL], solved, jnp.float32(0.0))
        done.append(solved)
        if panel_no == 0:
            rounded = solved.astype(jnp.bfloat16)
            work = strip[PANEL:] - contract_rows(rounded[:, PANEL:head], rounded)
    factors = jnp.concatenate(done, 0)
    rounded = factors.astype(jnp.bfloat16)
    mine = slice(head, head + rows_dev)
    left = jnp.concatenate([chosen[:, mine], -rounded[:, mine]], 0)
    right = jnp.concatenate([chosen[:, head + rows_dev :], rounded[:, head + rows_dev :]], 0)
    matrix = contract_rows(left, right)
    rows_g = cols_g[mine]
    out_g = cols_g[head + rows_dev :]
    matrix = matrix + jnp.where(
        rows_g[:, None] == out_g[None, :], slack_rows[:, None], jnp.float32(0.0)
    )
    padded = jnp.pad(factors[:, mine].T, ((0, 0), (0, cols_dev - head)))
    return jnp.where(
        out_g[None, :] < head,
        padded,
        jnp.where(rows_g[:, None] < head, jnp.float32(0.0), matrix),
    )


def solution(mesh):
    in_specs = (P("link", None, None), P("link", None), P("link"), P(), P())
    out_specs = P("link", "col")
    return jax.shard_map(local, mesh=mesh, in_specs=in_specs, out_specs=out_specs, check_vma=False)
```

time: 401 us -> 122 us (0.30)
  waiting for transfers between devices: 301 us -> 33.2 us
  starting transfers between devices: 6.98 us -> 0.01 us
  matrix products: 17.5 us -> 11.4 us
    psum x6 -> x0, waiting for transfers between devices: 270 us -> none  [spread_2(): return lax.psum(kept, axis)]
    all_gather x1, waiting for transfers between devices: 26.3 us -> 33.2 us  [local(): packed = lax.all_gather(packed, 'link', axis=0, tiled=True)]
    all_to_all x1 -> x0, starting transfers between devices: 6.55 us -> none  [local(): lax.all_to_all(own_dense, 'link', split_axis=1, concat_axis=0, tiled=True)]
    select_n x4 -> x0, other arithmetic: 5.7 us -> none  [spread_2(): jnp.where(lax.axis_index(axis) == source, value, 0).astype(value.dtype)]
    dot_general x6 -> x2, matrix products: 9.98 us -> 4.45 us  [the longest x1 4.26 us: local(): jnp.einsum('kjp,kju->kpu', onehot, all_vals, preferred_element_type=jnp.f...]
    all_to_all x1 -> x0, waiting for transfers between devices: 4.17 us -> none  [local(): lax.all_to_all(own_dense, 'link', split_axis=1, concat_axis=0, tiled=True)]
  transfers between devices with their start and end apart: 8 -> 1, of which waited for: 8 -> 1; matrix products, arithmetic and copies ran while one was open for 0% -> 4% of each run, Pallas kernels for 0% -> 0%
where the time goes in v1:
time: 122 us; the launch traced here: 120 us
  other arithmetic  54.3 us (45%)
  waiting for transfers between devices  33.2 us (27%)
  between operations  13.7 us (11%)
  matrix products  11.4 us (9%)
  local copies, waits for them, and re-layouts  7.27 us (6%)
    all_gather x1, waiting for transfers between devices, local(): packed = lax.all_gather(packed, 'link', axis=0, tiled=True)  33.2 us
    another operation x6, other arithmetic, local(): lower_fac = jnp.linalg.cholesky(work[:, first:first + PANEL])  25.1 us
    another operation x4, other arithmetic, local(): solved = jax.scipy.linalg.solve_triangular(lower_fac, work, lower=True)  21 us
    dot_general x1, matrix products, local(): jnp.einsum('kjp,kju->kpu', onehot, all_vals, preferred_element_type=jnp.f...  4.26 us
    another operation x2, matrix products, local(): solved = jax.scipy.linalg.solve_triangular(lower_fac, work, lower=True)  3.9 us
    dot_general x3, matrix products, contract_rows(): lax.dot_general(left_side, right_side, (((0,), (0,)), ((), ())), preferre...  3.07 us
    unnamed x24, local copies, waits for them, and re-layouts  2.63 us
  transfers between devices with their start and end apart: 1, of which 1 were waited for; matrix products, arithmetic and copies ran while one was open for 4% of the time, Pallas kernels for 0%

profile of v1, /device:TPU:11, one launch (start us, length us, event | category | flops | bytes accessed | tf_op | source)
XLA Modules:
  0.0 119.9 jit_solution(11520337397826129381)
XLA Ops:
  6.5 0.7 multiply_sqrt_fusion
  7.2 0.7 convert_element_type.37
  7.9 0.9 multiply_convert_fusion
  9.6 0.8 select_reduce_fusion.2
  13.6 1.2 iota_compare_fusion.1
  14.8 33.2 %all-gather.2.cloned.1.call-done = bf16[256,17,128]{2,0,1:T(8,128)(2,1)} async-done(((bf16[16,17,128]{2,0,1:T(8,128)(2,1)}), bf16[256,17,128]{2,0,1:T(8,128)(2,1)}) %all-gather.2.cloned.1.call-update) | async-done | bytes 1114128 | tf_op jit(solution)/shard_map/all_gather | solution.py:32
  48.0 0.9 fusion.23
  49.3 4.3 %fusion.8 = bf16[256,20,128]{2,1,0:T(8,128)(2,1)S(1)} fusion(bf16[256,16,128]{2,0,1:T(8,128)(2,1)S(1)} %slice-done, s32[20]{0:T(128)S(1)} %select_reduce_fusion.2, s32[256,16]{1,0:T(8,128)S(1)} %fusion.23), kind=kOutput, calls=%fused_computation.18 | convolution fusion | flops 21708800 | bytes 2375760 | tf_op jit(solution)/shard_map/kjp,kju->kpu/dot_general | solution.py:48
  53.5 1.2 %copy.32 = bf16[256,20,128]{0,2,1:T(8,128)(2,1)S(1)} copy(bf16[256,20,128]{2,1,0:T(8,128)(2,1)S(1)} %fusion.8) | data formatting | bytes 2621440 | tf_op jit(solution)/shard_map/convert_element_type | solution.py:49
  54.8 1.0 slice.109
  56.4 1.5 %copy-done.1 = f32[256,2560]{0,1:T(8,128)} copy-done((f32[256,2560]{0,1:T(8,128)}, f32[256,2560]{0,1:T(8,128)S(1)}, u32[]{:S(2)}) %copy-start.1) | copy-done | bytes 2621464
  58.0 0.9 fusion.27
  58.9 11.7 %cholesky.44 = f32[128,128]{1,0:T(8,128)S(1)} custom-call(f32[128,128]{1,0:T(8,128)S(1)} %fusion.27), custom_call_target="Cholesky" | custom-call | tf_op jit(solution)/shard_map/jit(cholesky)/cholesky | solution.py:70
  70.7 0.7 compare_reduce_fusion.1
  71.3 0.6 fusion.21
  72.0 9.8 %custom-call.6 = f32[1,128,128]{1,2,0:T(8,128)S(1)} custom-call(f32[1,128,128]{2,1,0:T(8,128)S(1)} %fusion.21), custom_call_target="InvertDiagBlocksLowerTriangular" | custom-call | tf_op jit(solution)/shard_map/jit(_solve_triangular)/triangular_solve | solution.py:71
  81.8 2.7 %fusion.34 = (bf16[128,2560]{0,1:T(8,128)(2,1)S(1)}, f32[128,2560]{0,1:T(8,128)S(1)}) fusion(f32[256,2560]{0,1:T(8,128)} %copy-done.1, f32[1,128,128]{1,2,0:T(8,128)S(1)} %custom-call.6, pred[256,2560]{0,1:T(32,128)(4,1)S(1)} %iota_compare_fusion.1), kind=kOutput, calls=%fused_computation.72 | convolution fusion | flops 503971840 | bytes 3670016 | tf_op jit(solution)/shard_map/jit(_solve_triangular)/triangular_solve | solution.py:71
  85.0 11.7 %cholesky.55 = f32[128,128]{1,0:T(8,128)S(1)} custom-call(f32[128,128]{1,0:T(8,128)S(1)} %fusion.25), custom_call_target="Cholesky" | custom-call | tf_op jit(solution)/shard_map/jit(cholesky)/cholesky | solution.py:70
  96.9 0.7 compare_reduce_fusion
  97.6 0.7 fusion.22
  98.4 9.8 %custom-call.7 = f32[1,128,128]{1,2,0:T(8,128)S(1)} custom-call(f32[1,128,128]{2,1,0:T(8,128)S(1)} %fusion.22), custom_call_target="InvertDiagBlocksLowerTriangular" | custom-call | tf_op jit(solution)/shard_map/jit(_solve_triangular)/triangular_solve | solution.py:71
  108.2 1.2 %convolution_select_fusion = f32[128,2560]{0,1:T(8,128)S(1)} fusion(f32[128,2560]{0,1:T(8,128)S(1)} %convolution_subtract_fusion, pred[256,2560]{0,1:T(32,128)(4,1)S(1)} %iota_compare_fusion.1, f32[1,128,128]{1,2,0:T(8,128)S(1)} %custom-call.7), kind=kOutput, calls=%fused_computation.1 | convolution fusion | flops 503644160 | bytes 3014656 | tf_op jit(solution)/shard_map/jit(_solve_triangular)/triangular_solve | solution.py:71
  109.7 1.1 copy-done.3
  110.8 2.2 %fusion.1 = f32[256,2048]{1,0:T(8,128)} fusion(bf16[256,2048]{0,1:T(8,128)(2,1)S(1)} %slice.110, bf16[256,2048]{0,1:T(8,128)(2,1)S(1)} %copy-done.3, f32[256,256]{1,0:T(8,128)S(1)} %fusion.16, f32[256]{0:T(256)S(1)} %copy-done.10, s32[2048]{0:T(1024)S(1)} %copy-done.7, s32[256]{0:T(256)S(1)} %copy-done.9, pred[256]{0:T(512)(128)(4,1)S(1)} %copy-done.11, ...), kind=kOutput, calls=%fused_computation.9 | convolution fusion | flops 544210944 | bytes 4731136 | tf_op jit(solution)/shard_map/dot_general | solution.py:10
  (53 shorter events, 5.9 us)
Async XLA Ops:
  6.5 3.9 %copy-start = (f32[4096]{0:T(1024)S(1)}, f32[4096]{0:T(1024)}, u32[]{:S(2)}) copy-start(f32[4096]{0:T(1024)} %param.11) | copy-start | bytes 49156
  6.5 41.5 %all-gather.2.cloned.1.call-start = ((), (), s32[]{:S(2)}) async-start(), calls=%async_computation | async-start | bytes 1183744 | tf_op jit(solution)/shard_map/all_gather | solution.py:32
  11.3 2.3 %copy-start.4 = (s32[2560]{0:T(1024)}, s32[2560]{0:T(1024)S(1)}, u32[]{:S(2)}) copy-start(s32[2560]{0:T(1024)S(1)} %get-tuple-element.12) | copy-start | bytes 30724
  48.0 1.3 %slice-start = ((bf16[256,17,128]{2,0,1:T(8,128)(2,1)}), bf16[256,16,128]{2,0,1:T(8,128)(2,1)S(1)}, s32[]{:S(2)}) async-start(bf16[256,17,128]{2,0,1:T(8,128)(2,1)} %all-gather.2.cloned.1.call-done), calls=%async_computation.1 | async-start | bytes 2097152 | tf_op jit(solution)/shard_map/slice | solution.py:33
  54.8 1.1 copy-start.5
  54.8 1.1 copy-start.6
  56.4 1.5 %copy-start.1 = (f32[256,2560]{0,1:T(8,128)}, f32[256,2560]{0,1:T(8,128)S(1)}, u32[]{:S(2)}) copy-start(f32[256,2560]{0,1:T(8,128)S(1)} %convolution_add_fusion) | copy-start | bytes 7864324
  81.8 2.7 %copy-start.2 = (f32[256,2560]{0,1:T(8,128)S(1)}, f32[256,2560]{0,1:T(8,128)}, u32[]{:S(2)}) copy-start(f32[256,2560]{0,1:T(8,128)} %copy-done.1) | copy-start | bytes 7864324
  109.6 1.2 %copy-start.3 = (bf16[256,2048]{0,1:T(8,128)(2,1)S(1)}, bf16[256,2048]{0,1:T(8,128)(2,1)}, u32[]{:S(2)}) copy-start(bf16[256,2048]{0,1:T(8,128)(2,1)} %slice.109) | copy-start | bytes 3145732
  109.6 1.2 %copy-start.7 = (s32[2048]{0:T(1024)S(1)}, s32[2048]{0:T(1024)}, u32[]{:S(2)}) copy-start(s32[2048]{0:T(1024)} %slice_bitcast_fusion.1) | copy-start | bytes 24580
  109.6 1.2 %copy-start.8 = (pred[2048]{0:T(1024)(128)(4,1)S(1)}, pred[2048]{0:T(1024)(128)(4,1)}, u32[]{:S(2)}) copy-start(pred[2048]{0:T(1024)(128)(4,1)} %broadcast_compare_fusion) | copy-start | bytes 6148
  109.6 1.2 %copy-start.9 = (s32[256]{0:T(256)S(1)}, s32[256]{0:T(256)}, u32[]{:S(2)}) copy-start(s32[256]{0:T(256)} %slice_bitcast_fusion.2) | copy-start | bytes 3076
  109.6 1.2 copy-start.10
  109.6 1.2 copy-start.11
Sparse Core Ops, SparseCore 0:
  9.6 38.3 all-gather.1

commit v2 on v1

--- a/solution.py
+++ b/solution.py
@@ -1,15 +1,71 @@
 import jax
 import jax.numpy as jnp
 from jax import lax
+from jax.experimental import pallas as pl
+from jax.experimental.pallas import tpu as pltpu
 from jax.sharding import PartitionSpec as P
 
 PANEL = 128
+STEP = 4
 
 
 def contract_rows(left_side, right_side):
     return lax.dot_general(
         left_side, right_side, (((0,), (0,)), ((), ())), preferred_element_type=jnp.float32
     )
+
+
+def inverse_kernel(block_ref, out_ref):
+    size = PANEL
+    row_ids = lax.broadcasted_iota(jnp.int32, (size, size), 0)
+    col_ids = lax.broadcasted_iota(jnp.int32, (size, size), 1)
+    left = block_ref[...]
+    right = (row_ids == col_ids).astype(jnp.float32)
+    for first in range(0, size, STEP):
+        inner = first % 8
+        if inner == 0 and first > 0:
+            left, right = left[8:], right[8:]
+        lefts = [left[inner + t : inner + t + 1] for t in range(STEP)]
+        rights = [right[inner + t : inner + t + 1] for t in range(STEP)]
+        small = {
+            (t, s): jnp.broadcast_to(lefts[t][:, first + s : first + s + 1], (1, size))
+            for t in range(STEP)
+            for s in range(t, STEP)
+        }
+        ratio, flipped = {}, []
+        for t in range(STEP):
+            flipped.append(1.0 / small[t, t])
+            for s in range(t + 1, STEP):
+                ratio[t, s] = small[t, s] * flipped[t]
+                for u in range(s, STEP):
+                    small[s, u] = small[s, u] - ratio[t, s] * small[t, u]
+                lefts[s] = lefts[s] - ratio[t, s] * lefts[t]
+                rights[s] = rights[s] - ratio[t, s] * rights[t]
+        for t in range(STEP):
+            out_ref[first + t : first + t + 1, :] = rights[t] * lax.rsqrt(small[t, t])
+        if first + STEP == size:
+            break
+        lefts = [lefts[t] * flipped[t] for t in range(STEP)]
+        rights = [rights[t] * flipped[t] for t in range(STEP)]
+        for t in range(STEP - 2, -1, -1):
+            for s in range(t + 1, STEP):
+                lefts[t] = lefts[t] - ratio[t, s] * lefts[s]
+                rights[t] = rights[t] - ratio[t, s] * rights[s]
+        spread = [
+            jnp.broadcast_to(left[:, first + t : first + t + 1], left.shape) for t in range(STEP)
+        ]
+        for t in range(STEP):
+            left = left - spread[t] * lefts[t]
+            right = right - spread[t] * rights[t]
+
+
+def inverse_factor(block):
+    return pl.pallas_call(
+        inverse_kernel,
+        out_shape=jax.ShapeDtypeStruct((PANEL, PANEL), jnp.float32),
+        in_specs=[pl.BlockSpec(memory_space=pltpu.VMEM)],
+        out_specs=pl.BlockSpec(memory_space=pltpu.VMEM),
+    )(block)
 
 
 def local(values, tiles, barrier, slack, order):
@@ -67,8 +123,8 @@
     work = strip[:PANEL]
     for panel_no in range(2):
         first = panel_no * PANEL
-        lower_fac = jnp.linalg.cholesky(work[:, first : first + PANEL])
-        solved = jax.scipy.linalg.solve_triangular(lower_fac, work, lower=True)
+        lower_inv = inverse_factor(work[:, first : first + PANEL])
+        solved = jnp.dot(lower_inv, work, precision=lax.Precision.HIGHEST)
         solved = jnp.where(keep[first : first + PANEL], solved, jnp.float32(0.0))
         done.append(solved)
         if panel_no == 0:

time: 122 us -> 94.3 us (0.77)
  other arithmetic: 54.3 us -> 7.27 us
  Pallas kernels: 0 us -> 13.4 us
  local copies, waits for them, and re-layouts: 7.27 us -> 11.3 us
  matrix products: 11.4 us -> 12.8 us
    another operation x10 -> x0, other arithmetic: 46.1 us -> none  [the longest x6 25.1 us: local(): lower_fac = jnp.linalg.cholesky(work[:, first:first + PANEL])]
    pallas_call x0 -> x2, Pallas kernels: none -> 13.4 us  [inverse_factor(): pl.pallas_call(inverse_kernel, out_shape=jax.ShapeDtypeStruct((PANEL, PAN...]
    dot_general x0 -> x2, matrix products: none -> 4.95 us  [local(): solved = jnp.dot(lower_inv, work, precision=lax.Precision.HIGHEST)]
    another operation x2 -> x0, matrix products: 3.9 us -> none  [local(): solved = jax.scipy.linalg.solve_triangular(lower_fac, work, lower=True)]
    select_n x0 -> x1, local copies, waits for them, and re-layouts: none -> 1.81 us  [local(): jnp.where(out_g[None, :] < head, padded, jnp.where(rows_g[:, None] < head...]
    unnamed x24 -> x16, local copies, waits for them, and re-layouts: 2.63 us -> 4.01 us
  transfers between devices with their start and end apart: 1 -> 1, of which waited for: 1 -> 1; matrix products, arithmetic and copies ran while one was open for 4% -> 5% of each run, Pallas kernels for 0% -> 0%
where the time goes in v2:
time: 94.3 us; the launch traced here: 92.5 us
  waiting for transfers between devices  34.1 us (36%)
  between operations  13.6 us (14%)
  Pallas kernels  13.4 us (14%)
  matrix products  12.8 us (14%)
  local copies, waits for them, and re-layouts  11.3 us (12%)
  other arithmetic  7.27 us (8%)
    all_gather x1, waiting for transfers between devices, local(): packed = lax.all_gather(packed, 'link', axis=0, tiled=True)  34.1 us
    pallas_call x2, Pallas kernels, inverse_factor(): pl.pallas_call(inverse_kernel, out_shape=jax.ShapeDtypeStruct((PANEL, PAN...  13.4 us
    dot_general x2, matrix products, local(): solved = jnp.dot(lower_inv, work, precision=lax.Precision.HIGHEST)  4.95 us
    dot_general x1, matrix products, local(): jnp.einsum('kjp,kju->kpu', onehot, all_vals, preferred_element_type=jnp.f...  4.26 us
    unnamed x16, local copies, waits for them, and re-layouts  4.01 us
    dot_general x3, matrix products, contract_rows(): lax.dot_general(left_side, right_side, (((0,), (0,)), ((), ())), preferre...  3.41 us
  transfers between devices with their start and end apart: 1, of which 1 were waited for; matrix products, arithmetic and copies ran while one was open for 5% of the time, Pallas kernels for 0%

profile of v2, /device:TPU:11, one launch (start us, length us, event | category | flops | bytes accessed | tf_op | source)
XLA Modules:
  0.0 92.5 jit_solution(7618199752122456658)
XLA Ops:
  6.5 0.7 multiply_sqrt_fusion
  7.2 0.7 convert_element_type.37
  7.9 0.9 multiply_convert_fusion
  8.8 0.6 pad_maximum_fusion.1
  9.6 0.8 select_reduce_fusion
  10.7 0.6 slice_bitcast_fusion.3
  13.0 0.6 slice_bitcast_fusion.1
  13.9 34.1 %all-gather.2.cloned.1.call-done = bf16[256,17,128]{2,0,1:T(8,128)(2,1)} async-done(((bf16[16,17,128]{2,0,1:T(8,128)(2,1)}), bf16[256,17,128]{2,0,1:T(8,128)(2,1)}) %all-gather.2.cloned.1.call-update) | async-done | bytes 1114128 | tf_op jit(solution)/shard_map/all_gather | solution.py:88
  48.0 0.9 %fusion.21 = s32[256,16]{1,0:T(8,128)S(1)} fusion(bf16[256,17,128]{2,0,1:T(8,128)(2,1)} %all-gather.2.cloned.1.call-done), kind=kLoop, calls=%fused_computation.33 | loop fusion | flops 4096 | bytes 24576 | tf_op jit(solution)/shard_map/convert_element_type | solution.py:90
  49.3 4.3 %fusion.8 = bf16[256,20,128]{2,1,0:T(8,128)(2,1)S(1)} fusion(bf16[256,16,128]{2,0,1:T(8,128)(2,1)S(1)} %slice-done, s32[20]{0:T(128)S(1)} %select_reduce_fusion, s32[256,16]{1,0:T(8,128)S(1)} %fusion.21), kind=kOutput, calls=%fused_computation.18 | convolution fusion | flops 21708800 | bytes 2375760 | tf_op jit(solution)/shard_map/kjp,kju->kpu/dot_general | solution.py:104
  53.5 1.0 %copy.23 = bf16[256,20,128]{0,2,1:T(8,128)(2,1)S(1)} copy(bf16[256,20,128]{2,1,0:T(8,128)(2,1)S(1)} %fusion.8) | data formatting | bytes 2621440 | tf_op jit(solution)/shard_map/convert_element_type | solution.py:105
  54.6 1.0 %slice.101 = bf16[256,2048]{0,1:T(8,128)(2,1)} slice(bf16[256,2560]{0,1:T(8,128)(2,1)S(1)} %bitcast.34), slice={[0:256], [512:2560]} | slice | bytes 2097152 | tf_op jit(solution)/shard_map/slice | solution.py:137
  56.2 1.5 %copy-done.1 = f32[256,2560]{1,0:T(8,128)} copy-done((f32[256,2560]{1,0:T(8,128)}, f32[256,2560]{1,0:T(8,128)S(1)}, u32[]{:S(2)}) %copy-start.1) | copy-done | bytes 2621464
  57.7 0.6 slice.90.block_ref
  58.4 6.7 %shard_map.55 = f32[128,128]{1,0:T(8,128)} custom-call(f32[128,128]{1,0:T(8,128)} %slice.90.block_ref), custom_call_target="tpu_custom_call" | custom-call | tf_op jit(solution)/shard_map/pallas_call | solution.py:63
  65.0 2.8 %fusion.28 = (bf16[128,2560]{1,0:T(8,128)(2,1)S(1)}, f32[128,2560]{1,0:T(8,128)S(1)}) fusion(f32[128,128]{1,0:T(8,128)} %shard_map.55, f32[256,2560]{1,0:T(8,128)} %copy-done.1, pred[256,2560]{1,0:T(32,128)(4,1)S(1)} %iota_compare_fusion.1), kind=kOutput, calls=%fused_computation.56 | convolution fusion | flops 503971840 | bytes 3670016 | tf_op jit(solution)/shard_map/dot_general | solution.py:127
  68.2 0.6 slice.95.block_ref
  68.8 6.7 %shard_map.56 = f32[128,128]{1,0:T(8,128)} custom-call(f32[128,128]{1,0:T(8,128)} %slice.95.block_ref), custom_call_target="tpu_custom_call" | custom-call | tf_op jit(solution)/shard_map/pallas_call | solution.py:63
  75.5 2.2 %convolution_select_fusion = f32[128,2560]{1,0:T(8,128)S(1)} fusion(f32[128,128]{1,0:T(8,128)} %shard_map.56, f32[128,2560]{1,0:T(8,128)S(1)} %convolution_subtract_fusion, pred[256,2560]{1,0:T(32,128)(4,1)S(1)} %iota_compare_fusion.1), kind=kOutput, calls=%fused_computation.1 | convolution fusion | flops 503644160 | bytes 3014656 | tf_op jit(solution)/shard_map/dot_general | solution.py:127
  77.7 0.7 fusion.16
  78.9 1.0 %copy-done.3 = bf16[256,2048]{0,1:T(8,128)(2,1)S(1)} copy-done((bf16[256,2048]{0,1:T(8,128)(2,1)S(1)}, bf16[256,2048]{0,1:T(8,128)(2,1)}, u32[]{:S(2)}) %copy-start.3) | copy-done | bytes 1048600
  79.9 1.4 %copy.31 = bf16[256,2048]{1,0:T(8,128)(2,1)} copy(bf16[256,2048]{0,1:T(8,128)(2,1)S(1)} %copy-done.3) | data formatting | bytes 2097152
  81.3 2.5 %fusion.1 = f32[256,2048]{0,1:T(8,128)S(1)} fusion(bf16[256,2048]{1,0:T(8,128)(2,1)S(1)} %slice.102, bf16[256,2048]{1,0:T(8,128)(2,1)} %copy.31, f32[256,256]{0,1:T(8,128)} %fusion.16, f32[256]{0:T(256)} %get-tuple-element.7, s32[256]{0:T(256)} %slice_bitcast_fusion.2, s32[2048]{0:T(1024)} %slice_bitcast_fusion.1, ...), kind=kOutput, calls=%fused_computation.9 | convolution fusion | flops 544210944 | bytes 4731136 | tf_op jit(solution)/shard_map/dot_general | solution.py:13
  83.8 1.8 %copy.27 = f32[256,2048]{1,0:T(8,128)} copy(f32[256,2048]{0,1:T(8,128)S(1)} %fusion.1) | data formatting | bytes 4194304 | tf_op jit(solution)/shard_map/jit(_where)/select_n | solution.py:145
  (34 shorter events, 4.1 us)
Async XLA Ops:
  6.5 3.9 %copy-start = (f32[4096]{0:T(1024)S(1)}, f32[4096]{0:T(1024)}, u32[]{:S(2)}) copy-start(f32[4096]{0:T(1024)} %param.8) | copy-start | bytes 49156
  6.5 41.5 %all-gather.2.cloned.1.call-start = ((), (), s32[]{:S(2)}) async-start(), calls=%async_computation | async-start | bytes 1183744 | tf_op jit(solution)/shard_map/all_gather | solution.py:88
  11.3 2.3 %copy-start.4 = (s32[2560]{0:T(1024)}, s32[2560]{0:T(1024)S(1)}, u32[]{:S(2)}) copy-start(s32[2560]{0:T(1024)S(1)} %get-tuple-element.10) | copy-start | bytes 30724
  48.0 1.3 %slice-start = ((bf16[256,17,128]{2,0,1:T(8,128)(2,1)}), bf16[256,16,128]{2,0,1:T(8,128)(2,1)S(1)}, s32[]{:S(2)}) async-start(bf16[256,17,128]{2,0,1:T(8,128)(2,1)} %all-gather.2.cloned.1.call-done), calls=%async_computation.1 | async-start | bytes 2097152 | tf_op jit(solution)/shard_map/slice | solution.py:89
  54.6 1.1 %copy-start.5 = (s32[2560]{0:T(1024)S(1)}, s32[2560]{0:T(1024)}, u32[]{:S(2)}) copy-start(s32[2560]{0:T(1024)} %copy-done.4) | copy-start | bytes 30724
  54.6 1.1 %copy-start.6 = (f32[256]{0:T(256)S(1)}, f32[256]{0:T(256)}, u32[]{:S(2)}) copy-start(f32[256]{0:T(256)} %get-tuple-element.8) | copy-start | bytes 3076
  56.2 1.5 %copy-start.1 = (f32[256,2560]{1,0:T(8,128)}, f32[256,2560]{1,0:T(8,128)S(1)}, u32[]{:S(2)}) copy-start(f32[256,2560]{1,0:T(8,128)S(1)} %convolution_add_fusion) | copy-start | bytes 7864324
  65.0 2.8 %copy-start.2 = (f32[256,2560]{1,0:T(8,128)S(1)}, f32[256,2560]{1,0:T(8,128)}, u32[]{:S(2)}) copy-start(f32[256,2560]{1,0:T(8,128)} %copy-done.1) | copy-start | bytes 7864324
  78.6 1.2 %copy-start.3 = (bf16[256,2048]{0,1:T(8,128)(2,1)S(1)}, bf16[256,2048]{0,1:T(8,128)(2,1)}, u32[]{:S(2)}) copy-start(bf16[256,2048]{0,1:T(8,128)(2,1)} %slice.101) | copy-start | bytes 3145732
Sparse Core Ops, SparseCore 0:
  9.6 38.3 all-gather.1

commit v3 on v2

--- a/solution.py
+++ b/solution.py
@@ -1,3 +1,5 @@
+import functools
+
 import jax
 import jax.numpy as jnp
 from jax import lax
@@ -68,6 +70,63 @@
     )(block)
 
 
+def gather_kernel(n, own_ref, out_ref, send_sem, pass_sem, recv_sem):
+    me = lax.axis_index("link")
+    core = me % 2
+    other = me + 1 - 2 * core
+    chip = me // 2
+    chips = n // 2
+    peers = [((chip + step) % chips) * 2 + core for step in range(1, chips)]
+    barrier = pltpu.get_barrier_semaphore()
+    for peer in peers + [other]:
+        pl.semaphore_signal(
+            barrier, inc=1, device_id={"link": peer}, device_id_type=pl.DeviceIdType.MESH
+        )
+    pl.semaphore_wait(barrier, chips)
+
+    def move(src, owner, send, target):
+        return pltpu.make_async_remote_copy(
+            src_ref=src,
+            dst_ref=out_ref.at[owner],
+            send_sem=send,
+            recv_sem=recv_sem.at[owner],
+            device_id={"link": target},
+            device_id_type=pl.DeviceIdType.MESH,
+        )
+
+    sent = [move(own_ref, me, send_sem.at[i], peer) for i, peer in enumerate(peers + [other])]
+    for copy in sent:
+        copy.start()
+    out_ref[me] = own_ref[...]
+    passed = []
+    for step in range(1, chips):
+        owner = ((chip + chips - step) % chips) * 2 + core
+        copy = move(out_ref.at[owner], owner, pass_sem.at[step], other)
+        copy.wait_recv()
+        copy.start()
+        passed.append(copy)
+    for step in range(chips):
+        owner = ((chip + chips - step) % chips) * 2 + 1 - core
+        move(own_ref, owner, send_sem.at[0], other).wait_recv()
+    for copy in sent + passed:
+        copy.wait_send()
+
+
+def gather_blocks(own, n):
+    return pl.pallas_call(
+        functools.partial(gather_kernel, n),
+        out_shape=jax.ShapeDtypeStruct((n,) + own.shape, own.dtype),
+        in_specs=[pl.BlockSpec(memory_space=pltpu.VMEM)],
+        out_specs=pl.BlockSpec(memory_space=pltpu.VMEM),
+        scratch_shapes=[
+            pltpu.SemaphoreType.DMA((n // 2,)),
+            pltpu.SemaphoreType.DMA((n // 2,)),
+            pltpu.SemaphoreType.DMA((n,)),
+        ],
+        compiler_params=pltpu.CompilerParams(collective_id=0, has_side_effects=True),
+    )(own)
+
+
 def local(values, tiles, barrier, slack, order):
     link_devs = lax.axis_size("link")
     col_devs = lax.axis_size("col")
@@ -84,10 +143,11 @@
         jnp.bfloat16
     )
     ids = jnp.pad(tiles.astype(jnp.bfloat16), ((0, 0), (0, tile_len - tpc)))
-    packed = jnp.concatenate([scaled, ids[:, None, :]], 1)
-    packed = lax.all_gather(packed, "link", axis=0, tiled=True)
-    all_vals = packed[:, :tpc]
-    all_ids = packed[:, tpc, :tpc].astype(jnp.int32)
+    per_dev = values.shape[0]
+    packed = jnp.concatenate([scaled.reshape(per_dev * tpc, tile_len), ids], 0)
+    packed = gather_blocks(packed, link_devs)
+    all_vals = packed[:, : per_dev * tpc].reshape(-1, tpc, tile_len)
+    all_ids = packed[:, per_dev * tpc :, :tpc].astype(jnp.int32).reshape(-1, tpc)
 
     row_tiles = rows_dev // tile_len
     col_tiles = cols_dev // tile_len

time: 94.3 us -> 61.1 us (0.65); the launches traced: 92.5 us -> 60.6 us
  waiting for transfers between devices: 34.1 us -> 0 us
  Pallas kernels: 13.4 us -> 33.4 us
  between operations: 13.6 us -> 0.26 us
  matrix products: 12.8 us -> 9.92 us
  other arithmetic: 7.27 us -> 5.62 us
    all_gather x1 -> x0, waiting for transfers between devices: 34.1 us -> none  [local(): packed = lax.all_gather(packed, 'link', axis=0, tiled=True)]
    pallas_call x0 -> x1, Pallas kernels: none -> 20.1 us  [gather_blocks(): pl.pallas_call(functools.partial(gather_kernel, n), out_shape=jax.ShapeDt...]
    dot_general x1, matrix products: 4.26 us -> 2.68 us  [local(): jnp.einsum('kjp,kju->kpu', onehot, all_vals, preferred_element_type=jnp.f...]
    dot_general x3, matrix products: 3.41 us -> 2.1 us  [contract_rows(): lax.dot_general(left_side, right_side, (((0,), (0,)), ((), ())), preferre...]
    slice x1, local copies, waits for them, and re-layouts: 1.04 us -> 0.07 us  [local(): chosen[:, head + rows_dev:]]
    unnamed x16 -> x26, local copies, waits for them, and re-layouts: 4.01 us -> 4.09 us
  transfers between devices with their start and end apart: 1 -> 0, of which waited for: 1 -> 0; matrix products, arithmetic and copies ran while one was open for 5% -> 0% of each run, Pallas kernels for 0% -> 0%
where the time goes in v3:
time: 61.1 us; the launch traced here: 60.6 us
  Pallas kernels  33.4 us (55%)
  local copies, waits for them, and re-layouts  11.4 us (19%)
  matrix products  9.92 us (16%)
  other arithmetic  5.62 us (9%)
    pallas_call x1, Pallas kernels, gather_blocks(): pl.pallas_call(functools.partial(gather_kernel, n), out_shape=jax.ShapeDt...  20.1 us
    pallas_call x2, Pallas kernels, inverse_factor(): pl.pallas_call(inverse_kernel, out_shape=jax.ShapeDtypeStruct((PANEL, PAN...  13.4 us
    dot_general x2, matrix products, local(): solved = jnp.dot(lower_inv, work, precision=lax.Precision.HIGHEST)  4.95 us
    unnamed x26, local copies, waits for them, and re-layouts  4.09 us
    dot_general x1, matrix products, local(): jnp.einsum('kjp,kju->kpu', onehot, all_vals, preferred_element_type=jnp.f...  2.68 us
    dot_general x3, matrix products, contract_rows(): lax.dot_general(left_side, right_side, (((0,), (0,)), ((), ())), preferre...  2.1 us
    select_n x1, local copies, waits for them, and re-layouts, local(): jnp.where(out_g[None, :] < head, padded, jnp.where(rows_g[:, None] < head...  1.81 us
    slice x2, local copies, waits for them, and re-layouts, local(): lower_inv = inverse_factor(work[:, first:first + PANEL])  1.25 us

profile of v3, /device:TPU:11, one launch (start us, length us, event | category | flops | bytes accessed | tf_op | source)
XLA Modules:
  0.0 60.6 jit_solution(3799837993160137281)
XLA Ops:
  0.0 0.7 %multiply_sqrt_fusion = f32[16]{0:T(128)S(1)} fusion(f32[16]{0:T(128)} %param.7), kind=kLoop, calls=%fused_computation.50 | loop fusion | flops 16 | bytes 128 | tf_op jit(solution)/shard_map/sqrt | solution.py:142
  0.8 0.8 %select_reduce_fusion = s32[20]{0:T(128)S(1)} fusion(s32[32]{0:T(128)} %param.9, s32[20]{0:T(128)S(1)} %get-tuple-element.6), kind=kLoop, calls=%fused_computation.37 | loop fusion | flops 1900 | bytes 288 | tf_op jit(solution)/shard_map/reduce_sum | solution.py:162
  1.8 0.6 slice_bitcast_fusion.2
  2.4 0.7 %convert_element_type.28 = bf16[16,16]{1,0:T(8,128)(2,1)S(1)} convert(s32[16,16]{1,0:T(8,128)} %param.6) | non-fusion elementwise | flops 256 | bytes 1536 | tf_op jit(solution)/shard_map/convert_element_type | solution.py:145
  3.7 0.6 slice_bitcast_fusion.1
  4.8 0.6 slice_bitcast_fusion
  5.4 0.9 %multiply_convert_fusion = bf16[16,16,128]{2,1,0:T(8,128)(2,1)S(1)} fusion(bf16[16,16,128]{2,1,0:T(8,128)(2,1)} %param.5, f32[16]{0:T(128)S(1)} %multiply_sqrt_fusion), kind=kLoop, calls=%fused_computation.31 | loop fusion | flops 98304 | bytes 131136 | tf_op jit(solution)/shard_map/convert_element_type | solution.py:142
  6.4 0.6 %fusion.21.own_ref = bf16[272,128]{1,0:T(8,128)(2,1)} fusion(bf16[16,16]{1,0:T(8,128)(2,1)S(1)} %convert_element_type.28, bf16[256,128]{1,0:T(8,128)(2,1)S(1)} %bitcast.36), kind=kLoop, calls=%fused_computation.32 | loop fusion | flops 208896 | bytes 135680 | tf_op jit(solution)/shard_map/concatenate | solution.py:147
  7.3 20.1 %shard_map.55 = bf16[16,272,128]{2,1,0:T(8,128)(2,1)} custom-call(bf16[272,128]{1,0:T(8,128)(2,1)} %fusion.21.own_ref), custom_call_target="tpu_custom_call" | custom-call | tf_op jit(solution)/shard_map/pallas_call | solution.py:116
  27.4 0.9 %slice.67 = bf16[16,16,16]{2,1,0:T(8,128)(2,1)S(1)} slice(bf16[16,272,128]{2,1,0:T(8,128)(2,1)} %shard_map.55), slice={[0:16], [256:272], [0:16]} | slice | bytes 16384 | tf_op jit(solution)/shard_map/slice | solution.py:150
  28.7 2.7 %fusion.8 = bf16[256,20,128]{2,1,0:T(8,128)(2,1)S(1)} fusion(bf16[256,16,128]{2,1,0:T(8,128)(2,1)S(1)} %bitcast.35, s32[20]{0:T(128)S(1)} %select_reduce_fusion, s32[256,16]{1,0:T(8,128)S(1)} %bitcast_convert_fusion), kind=kOutput, calls=%fused_computation.18 | convolution fusion | flops 21708800 | bytes 2375760 | tf_op jit(solution)/shard_map/kjp,kju->kpu/dot_general | solution.py:164
  31.4 1.0 %copy.13 = bf16[256,20,128]{0,2,1:T(8,128)(2,1)S(1)} copy(bf16[256,20,128]{2,1,0:T(8,128)(2,1)S(1)} %fusion.8) | data formatting | bytes 2621440 | tf_op jit(solution)/shard_map/convert_element_type | solution.py:165
  32.6 1.4 %copy.20 = bf16[256,2048]{1,0:T(8,128)(2,1)} copy(bf16[256,2048]{0,1:T(8,128)(2,1)S(1)} %slice.99) | data formatting | bytes 2097152
  34.1 0.5 convolution_add_fusion
  34.6 1.5 %copy-done.1 = f32[256,2560]{1,0:T(8,128)} copy-done((f32[256,2560]{1,0:T(8,128)}, f32[256,2560]{1,0:T(8,128)S(1)}, u32[]{:S(2)}) %copy-start.1) | copy-done | bytes 2621464
  36.1 0.6 %slice.88.block_ref = f32[128,128]{1,0:T(8,128)} slice(f32[256,2560]{1,0:T(8,128)S(1)} %convolution_add_fusion), slice={[0:128], [0:128]} | slice | bytes 131072 | tf_op jit(solution)/shard_map/slice | solution.py:186
  36.7 6.7 %shard_map.56 = f32[128,128]{1,0:T(8,128)} custom-call(f32[128,128]{1,0:T(8,128)} %slice.88.block_ref), custom_call_target="tpu_custom_call" | custom-call | tf_op jit(solution)/shard_map/pallas_call | solution.py:65
  43.4 2.8 %fusion.28 = (bf16[128,2560]{1,0:T(8,128)(2,1)S(1)}, f32[128,2560]{1,0:T(8,128)S(1)}) fusion(f32[128,128]{1,0:T(8,128)} %shard_map.56, f32[256,2560]{1,0:T(8,128)} %copy-done.1, pred[256,2560]{1,0:T(32,128)(4,1)S(1)} %iota_compare_fusion.1), kind=kOutput, calls=%fused_computation.55 | convolution fusion | flops 503971840 | bytes 3670016 | tf_op jit(solution)/shard_map/dot_general | solution.py:187
  46.6 0.6 %slice.93.block_ref = f32[128,128]{1,0:T(8,128)} slice(f32[128,2560]{1,0:T(8,128)S(1)} %convolution_subtract_fusion), slice={[0:128], [128:256]} | slice | bytes 131072 | tf_op jit(solution)/shard_map/slice | solution.py:186
  47.2 6.7 %shard_map.57 = f32[128,128]{1,0:T(8,128)} custom-call(f32[128,128]{1,0:T(8,128)} %slice.93.block_ref), custom_call_target="tpu_custom_call" | custom-call | tf_op jit(solution)/shard_map/pallas_call | solution.py:65
  53.9 2.2 %convolution_select_fusion = f32[128,2560]{1,0:T(8,128)S(1)} fusion(f32[128,128]{1,0:T(8,128)} %shard_map.57, f32[128,2560]{1,0:T(8,128)S(1)} %convolution_subtract_fusion, pred[256,2560]{1,0:T(32,128)(4,1)S(1)} %iota_compare_fusion.1), kind=kOutput, calls=%fused_computation.1 | convolution fusion | flops 503644160 | bytes 3014656 | tf_op jit(solution)/shard_map/dot_general | solution.py:187
  56.5 1.0 %copy-done.3 = bf16[256,2048]{1,0:T(8,128)(2,1)S(1)} copy-done((bf16[256,2048]{1,0:T(8,128)(2,1)S(1)}, bf16[256,2048]{1,0:T(8,128)(2,1)}, u32[]{:S(2)}) %copy-start.3) | copy-done | bytes 1048600
  57.6 1.2 %fusion.1 = f32[256,2048]{0,1:T(8,128)S(1)} fusion(bf16[256,2048]{1,0:T(8,128)(2,1)S(1)} %slice.100, bf16[256,2048]{1,0:T(8,128)(2,1)S(1)} %copy-done.3, f32[256,256]{0,1:T(8,128)S(1)} %fusion.15, f32[256]{0:T(256)S(1)} %copy-done.10, s32[256]{0:T(256)S(1)} %copy-done.9, s32[2048]{0:T(1024)S(1)} %copy-done.6, pred[2048]{0:T(1024)(128)(4,1)S(1)} %copy-done.8, ...), kind=kOutput, calls=%fused_computation.9 | convolution fusion | flops 544210944 | bytes 4731136 | tf_op jit(solution)/shard_map/dot_general | solution.py:15
  58.8 1.8 %copy.17 = f32[256,2048]{1,0:T(8,128)} copy(f32[256,2048]{0,1:T(8,128)S(1)} %fusion.1) | data formatting | bytes 4194304 | tf_op jit(solution)/shard_map/jit(_where)/select_n | solution.py:205
  (42 shorter events, 3.0 us)
Async XLA Ops:
  0.0 1.6 %copy-start = (f32[4096]{0:T(1024)S(1)}, f32[4096]{0:T(1024)}, u32[]{:S(2)}) copy-start(f32[4096]{0:T(1024)} %param.8) | copy-start | bytes 49156
  3.2 3.8 %copy-start.4 = (s32[2560]{0:T(1024)}, s32[2560]{0:T(1024)S(1)}, u32[]{:S(2)}) copy-start(s32[2560]{0:T(1024)S(1)} %get-tuple-element.10) | copy-start | bytes 30724
  27.4 1.3 %slice-start = ((bf16[16,272,128]{2,1,0:T(8,128)(2,1)}), bf16[16,256,128]{2,1,0:T(8,128)(2,1)S(1)}, s32[]{:S(2)}) async-start(bf16[16,272,128]{2,1,0:T(8,128)(2,1)} %shard_map.55), calls=%async_computation | async-start | bytes 2097152 | tf_op jit(solution)/shard_map/slice | solution.py:149
  32.5 1.5 %copy-start.5 = (s32[2560]{0:T(1024)S(1)}, s32[2560]{0:T(1024)}, u32[]{:S(2)}) copy-start(s32[2560]{0:T(1024)} %copy-done.4) | copy-start | bytes 30724
  32.5 1.5 %copy-start.7 = (f32[256]{0:T(256)S(1)}, f32[256]{0:T(256)}, u32[]{:S(2)}) copy-start(f32[256]{0:T(256)} %get-tuple-element.8) | copy-start | bytes 3076
  34.6 1.5 %copy-start.1 = (f32[256,2560]{1,0:T(8,128)}, f32[256,2560]{1,0:T(8,128)S(1)}, u32[]{:S(2)}) copy-start(f32[256,2560]{1,0:T(8,128)S(1)} %convolution_add_fusion) | copy-start | bytes 7864324
  43.4 2.8 %copy-start.2 = (f32[256,2560]{1,0:T(8,128)S(1)}, f32[256,2560]{1,0:T(8,128)}, u32[]{:S(2)}) copy-start(f32[256,2560]{1,0:T(8,128)} %copy-done.1) | copy-start | bytes 7864324
  56.3 1.2 %copy-start.3 = (bf16[256,2048]{1,0:T(8,128)(2,1)S(1)}, bf16[256,2048]{1,0:T(8,128)(2,1)}, u32[]{:S(2)}) copy-start(bf16[256,2048]{1,0:T(8,128)(2,1)} %copy.20) | copy-start | bytes 3145732
  56.3 1.2 %copy-start.6 = (s32[2048]{0:T(1024)S(1)}, s32[2048]{0:T(1024)}, u32[]{:S(2)}) copy-start(s32[2048]{0:T(1024)} %slice_bitcast_fusion) | copy-start | bytes 24580
  56.3 1.2 %copy-start.8 = (pred[2048]{0:T(1024)(128)(4,1)S(1)}, pred[2048]{0:T(1024)(128)(4,1)}, u32[]{:S(2)}) copy-start(pred[2048]{0:T(1024)(128)(4,1)} %broadcast_compare_fusion) | copy-start | bytes 6148
  56.4 1.2 %copy-start.9 = (s32[256]{0:T(256)S(1)}, s32[256]{0:T(256)}, u32[]{:S(2)}) copy-start(s32[256]{0:T(256)} %slice_bitcast_fusion.1) | copy-start | bytes 3076
  56.4 1.2 %copy-start.10 = (f32[256]{0:T(256)S(1)}, f32[256]{0:T(256)}, u32[]{:S(2)}) copy-start(f32[256]{0:T(256)} %get-tuple-element.7) | copy-start | bytes 3076
  56.4 1.2 %copy-start.11 = (pred[256]{0:T(512)(128)(4,1)S(1)}, pred[256]{0:T(512)(128)(4,1)}, u32[]{:S(2)}) copy-start(pred[256]{0:T(512)(128)(4,1)} %broadcast_compare_fusion.1) | copy-start | bytes 772

commit v4 on v3

--- a/solution.py
+++ b/solution.py
@@ -8,7 +8,7 @@
 from jax.sharding import PartitionSpec as P
 
 PANEL = 128
-STEP = 4
+STEP = 8
 
 
 def contract_rows(left_side, right_side):
@@ -165,11 +165,9 @@
     chosen = chosen.astype(jnp.bfloat16).reshape(all_vals.shape[0], -1)
     cols_g = (places[:, None] * tile_len + jnp.arange(tile_len)[None, :]).reshape(-1)
 
-    target_hot = (targets[: head // tile_len + row_tiles, None] == jnp.arange(ntiles)).astype(
-        jnp.float32
-    )
-    slack_some = jnp.dot(
-        target_hot, slack.reshape(ntiles, tile_len), precision=lax.Precision.HIGHEST
+    target_hot = targets[: head // tile_len + row_tiles, None] == jnp.arange(ntiles)[None, :]
+    slack_some = jnp.sum(
+        jnp.where(target_hot[:, :, None], slack.reshape(1, ntiles, tile_len), jnp.float32(0.0)), 1
     ).reshape(-1)
     slack_head, slack_rows = slack_some[:head], slack_some[head:]
 

time: 61.1 us -> 60.3 us (0.987)
  Pallas kernels: 33.4 us -> 31.9 us
  other arithmetic: 5.62 us -> 6.57 us
    pallas_call x2, Pallas kernels: 13.4 us -> 11.9 us  [inverse_factor(): pl.pallas_call(inverse_kernel, out_shape=jax.ShapeDtypeStruct((PANEL, PAN...]
    reduce_sum x0 -> x1, other arithmetic: none -> 0.82 us  [local(): jnp.sum(jnp.where(target_hot[:, :, None], slack.reshape(1, ntiles, tile_l...]
    unnamed x26 -> x18, local copies, waits for them, and re-layouts: 4.09 us -> 4.09 us
where the time goes in v4:
time: 60.3 us; the launch traced here: 59.8 us
  Pallas kernels  31.9 us (53%)
  local copies, waits for them, and re-layouts  11.3 us (19%)
  matrix products  9.73 us (16%)
  other arithmetic  6.57 us (11%)
    pallas_call x1, Pallas kernels, gather_blocks(): pl.pallas_call(functools.partial(gather_kernel, n), out_shape=jax.ShapeDt...  20.1 us
    pallas_call x2, Pallas kernels, inverse_factor(): pl.pallas_call(inverse_kernel, out_shape=jax.ShapeDtypeStruct((PANEL, PAN...  11.9 us
    dot_general x2, matrix products, local(): solved = jnp.dot(lower_inv, work, precision=lax.Precision.HIGHEST)  4.95 us
    unnamed x18, local copies, waits for them, and re-layouts  4.09 us
    dot_general x1, matrix products, local(): jnp.einsum('kjp,kju->kpu', onehot, all_vals, preferred_element_type=jnp.f...  2.68 us
    dot_general x3, matrix products, contract_rows(): lax.dot_general(left_side, right_side, (((0,), (0,)), ((), ())), preferre...  2.1 us
    select_n x1, local copies, waits for them, and re-layouts, local(): jnp.where(out_g[None, :] < head, padded, jnp.where(rows_g[:, None] < head...  1.81 us
    slice x2, local copies, waits for them, and re-layouts, local(): lower_inv = inverse_factor(work[:, first:first + PANEL])  1.28 us

profile of v4, /device:TPU:11, one launch (start us, length us, event | category | flops | bytes accessed | tf_op | source)
XLA Modules:
  0.0 59.8 jit_solution(5932205652577681473)
XLA Ops:
  0.0 0.7 %multiply_sqrt_fusion = f32[16]{0:T(128)S(1)} fusion(f32[16]{0:T(128)} %param.7), kind=kLoop, calls=%fused_computation.48 | loop fusion | flops 16 | bytes 128 | tf_op jit(solution)/shard_map/sqrt | solution.py:142
  0.8 0.8 %select_reduce_fusion.1 = s32[20]{0:T(128)S(1)} fusion(s32[32]{0:T(128)} %param.9, s32[20]{0:T(128)S(1)} %get-tuple-element.6), kind=kLoop, calls=%fused_computation.36 | loop fusion | flops 1900 | bytes 288 | tf_op jit(solution)/shard_map/reduce_sum | solution.py:162
  1.7 0.8 %select_reduce_fusion = f32[4,128]{1,0:T(4,128)S(1)} fusion(f32[32,128]{1,0:T(8,128)} %bitcast.35, pred[4,32]{1,0:T(4,128)(4,1)S(1)} %iota_compare_fusion.4), kind=kLoop, calls=%fused_computation.34 | loop fusion | flops 32256 | bytes 18560 | tf_op jit(solution)/shard_map/reduce_sum | solution.py:169
  2.5 0.6 slice_bitcast_fusion.2
  3.1 0.7 %convert_element_type.27 = bf16[16,16]{1,0:T(8,128)(2,1)S(1)} convert(s32[16,16]{1,0:T(8,128)} %param.6) | non-fusion elementwise | flops 256 | bytes 1536 | tf_op jit(solution)/shard_map/convert_element_type | solution.py:145
  4.9 0.6 broadcast_compare_fusion
  5.5 0.6 slice_bitcast_fusion
  6.1 0.9 %multiply_convert_fusion = bf16[16,16,128]{2,1,0:T(8,128)(2,1)S(1)} fusion(bf16[16,16,128]{2,1,0:T(8,128)(2,1)} %param.5, f32[16]{0:T(128)S(1)} %multiply_sqrt_fusion), kind=kLoop, calls=%fused_computation.31 | loop fusion | flops 98304 | bytes 131136 | tf_op jit(solution)/shard_map/convert_element_type | solution.py:142
  7.0 0.6 %fusion.21.own_ref = bf16[272,128]{1,0:T(8,128)(2,1)} fusion(bf16[16,16]{1,0:T(8,128)(2,1)S(1)} %convert_element_type.27, bf16[256,128]{1,0:T(8,128)(2,1)S(1)} %bitcast.34), kind=kLoop, calls=%fused_computation.32 | loop fusion | flops 208896 | bytes 135680 | tf_op jit(solution)/shard_map/concatenate | solution.py:147
  8.0 20.1 %shard_map.55 = bf16[16,272,128]{2,1,0:T(8,128)(2,1)} custom-call(bf16[272,128]{1,0:T(8,128)(2,1)} %fusion.21.own_ref), custom_call_target="tpu_custom_call" | custom-call | tf_op jit(solution)/shard_map/pallas_call | solution.py:116
  28.1 0.9 %slice.67 = bf16[16,16,16]{2,1,0:T(8,128)(2,1)S(1)} slice(bf16[16,272,128]{2,1,0:T(8,128)(2,1)} %shard_map.55), slice={[0:16], [256:272], [0:16]} | slice | bytes 16384 | tf_op jit(solution)/shard_map/slice | solution.py:150
  29.4 2.7 %fusion.8 = bf16[256,20,128]{2,1,0:T(8,128)(2,1)S(1)} fusion(bf16[256,16,128]{2,1,0:T(8,128)(2,1)S(1)} %bitcast.33, s32[20]{0:T(128)S(1)} %select_reduce_fusion.1, s32[256,16]{1,0:T(8,128)S(1)} %bitcast_convert_fusion), kind=kOutput, calls=%fused_computation.18 | convolution fusion | flops 21708800 | bytes 2375760 | tf_op jit(solution)/shard_map/kjp,kju->kpu/dot_general | solution.py:164
  32.0 1.0 %copy.13 = bf16[256,20,128]{0,2,1:T(8,128)(2,1)S(1)} copy(bf16[256,20,128]{2,1,0:T(8,128)(2,1)S(1)} %fusion.8) | data formatting | bytes 2621440 | tf_op jit(solution)/shard_map/convert_element_type | solution.py:165
  33.3 1.4 %copy.20 = bf16[256,2048]{1,0:T(8,128)(2,1)} copy(bf16[256,2048]{0,1:T(8,128)(2,1)S(1)} %slice.99) | data formatting | bytes 2097152
  35.3 1.5 %copy-done = f32[256,2560]{1,0:T(8,128)} copy-done((f32[256,2560]{1,0:T(8,128)}, f32[256,2560]{1,0:T(8,128)S(1)}, u32[]{:S(2)}) %copy-start) | copy-done | bytes 2621464
  36.8 0.6 %slice.88.block_ref = f32[128,128]{1,0:T(8,128)} slice(f32[256,2560]{1,0:T(8,128)S(1)} %convolution_add_fusion), slice={[0:128], [0:128]} | slice | bytes 131072 | tf_op jit(solution)/shard_map/slice | solution.py:184
  37.4 5.9 %shard_map.56 = f32[128,128]{1,0:T(8,128)} custom-call(f32[128,128]{1,0:T(8,128)} %slice.88.block_ref), custom_call_target="tpu_custom_call" | custom-call | tf_op jit(solution)/shard_map/pallas_call | solution.py:65
  43.3 2.8 %fusion.25 = (bf16[128,2560]{1,0:T(8,128)(2,1)S(1)}, f32[128,2560]{1,0:T(8,128)S(1)}) fusion(f32[128,128]{1,0:T(8,128)} %shard_map.56, f32[256,2560]{1,0:T(8,128)} %copy-done, pred[256,2560]{1,0:T(32,128)(4,1)S(1)} %iota_compare_fusion.1), kind=kOutput, calls=%fused_computation.53 | convolution fusion | flops 503971840 | bytes 3670016 | tf_op jit(solution)/shard_map/dot_general | solution.py:185
  46.5 0.6 %slice.93.block_ref = f32[128,128]{1,0:T(8,128)} slice(f32[128,2560]{1,0:T(8,128)S(1)} %convolution_subtract_fusion), slice={[0:128], [128:256]} | slice | bytes 131072 | tf_op jit(solution)/shard_map/slice | solution.py:184
  47.1 5.9 %shard_map.57 = f32[128,128]{1,0:T(8,128)} custom-call(f32[128,128]{1,0:T(8,128)} %slice.93.block_ref), custom_call_target="tpu_custom_call" | custom-call | tf_op jit(solution)/shard_map/pallas_call | solution.py:65
  53.1 2.2 %convolution_select_fusion = f32[128,2560]{1,0:T(8,128)S(1)} fusion(f32[128,128]{1,0:T(8,128)} %shard_map.57, f32[128,2560]{1,0:T(8,128)S(1)} %convolution_subtract_fusion, pred[256,2560]{1,0:T(32,128)(4,1)S(1)} %iota_compare_fusion.1), kind=kOutput, calls=%fused_computation.1 | convolution fusion | flops 503644160 | bytes 3014656 | tf_op jit(solution)/shard_map/dot_general | solution.py:185
  55.7 1.0 %copy-done.2 = bf16[256,2048]{1,0:T(8,128)(2,1)S(1)} copy-done((bf16[256,2048]{1,0:T(8,128)(2,1)S(1)}, bf16[256,2048]{1,0:T(8,128)(2,1)}, u32[]{:S(2)}) %copy-start.2) | copy-done | bytes 1048600
  56.7 1.2 %fusion.1 = f32[256,2048]{0,1:T(8,128)S(1)} fusion(bf16[256,2048]{1,0:T(8,128)(2,1)S(1)} %slice.100, bf16[256,2048]{1,0:T(8,128)(2,1)S(1)} %copy-done.2, f32[256,256]{0,1:T(8,128)S(1)} %fusion.15, f32[256]{0:T(256)S(1)} %copy-done.6, s32[256]{0:T(256)S(1)} %copy-done.5, s32[2048]{0:T(1024)S(1)} %copy-done.3, pred[2048]{0:T(1024)(128)(4,1)S(1)} %copy-done.4, ...), kind=kOutput, calls=%fused_computation.9 | convolution fusion | flops 544210944 | bytes 4731136 | tf_op jit(solution)/shard_map/dot_general | solution.py:15
  58.0 1.8 %copy.17 = f32[256,2048]{1,0:T(8,128)} copy(f32[256,2048]{0,1:T(8,128)S(1)} %fusion.1) | data formatting | bytes 4194304 | tf_op jit(solution)/shard_map/jit(_where)/select_n | solution.py:203
  (35 shorter events, 3.4 us)
Async XLA Ops:
  28.1 1.3 %slice-start = ((bf16[16,272,128]{2,1,0:T(8,128)(2,1)}), bf16[16,256,128]{2,1,0:T(8,128)(2,1)S(1)}, s32[]{:S(2)}) async-start(bf16[16,272,128]{2,1,0:T(8,128)(2,1)} %shard_map.55), calls=%async_computation | async-start | bytes 2097152 | tf_op jit(solution)/shard_map/slice | solution.py:149
  35.3 1.5 %copy-start = (f32[256,2560]{1,0:T(8,128)}, f32[256,2560]{1,0:T(8,128)S(1)}, u32[]{:S(2)}) copy-start(f32[256,2560]{1,0:T(8,128)S(1)} %convolution_add_fusion) | copy-start | bytes 7864324
  43.3 2.8 %copy-start.1 = (f32[256,2560]{1,0:T(8,128)S(1)}, f32[256,2560]{1,0:T(8,128)}, u32[]{:S(2)}) copy-start(f32[256,2560]{1,0:T(8,128)} %copy-done) | copy-start | bytes 7864324
  55.5 1.2 %copy-start.2 = (bf16[256,2048]{1,0:T(8,128)(2,1)S(1)}, bf16[256,2048]{1,0:T(8,128)(2,1)}, u32[]{:S(2)}) copy-start(bf16[256,2048]{1,0:T(8,128)(2,1)} %copy.20) | copy-start | bytes 3145732
  55.5 1.2 %copy-start.3 = (s32[2048]{0:T(1024)S(1)}, s32[2048]{0:T(1024)}, u32[]{:S(2)}) copy-start(s32[2048]{0:T(1024)} %slice_bitcast_fusion) | copy-start | bytes 24580
  55.5 1.2 %copy-start.4 = (pred[2048]{0:T(1024)(128)(4,1)S(1)}, pred[2048]{0:T(1024)(128)(4,1)}, u32[]{:S(2)}) copy-start(pred[2048]{0:T(1024)(128)(4,1)} %broadcast_compare_fusion) | copy-start | bytes 6148
  55.5 1.2 %copy-start.5 = (s32[256]{0:T(256)S(1)}, s32[256]{0:T(256)}, u32[]{:S(2)}) copy-start(s32[256]{0:T(256)} %slice_bitcast_fusion.1) | copy-start | bytes 3076
  55.5 1.2 %copy-start.6 = (f32[256]{0:T(256)S(1)}, f32[256]{0:T(256)}, u32[]{:S(2)}) copy-start(f32[256]{0:T(256)} %get-tuple-element.7) | copy-start | bytes 3076
  55.5 1.2 %copy-start.7 = (pred[256]{0:T(512)(128)(4,1)S(1)}, pred[256]{0:T(512)(128)(4,1)}, u32[]{:S(2)}) copy-start(pred[256]{0:T(512)(128)(4,1)} %broadcast_compare_fusion.1) | copy-start | bytes 772

commit v5 on v4

--- a/solution.py
+++ b/solution.py
@@ -163,7 +163,18 @@
     onehot = (all_ids[:, :, None] == targets[None, None, :]).astype(jnp.bfloat16)
     chosen = jnp.einsum("kjp,kju->kpu", onehot, all_vals, preferred_element_type=jnp.float32)
     chosen = chosen.astype(jnp.bfloat16).reshape(all_vals.shape[0], -1)
-    cols_g = (places[:, None] * tile_len + jnp.arange(tile_len)[None, :]).reshape(-1)
+    rows_g = link_idx * rows_dev + jnp.arange(rows_dev)
+    out_g = col_idx * cols_dev + jnp.arange(cols_dev)
+    at = jnp.arange(head + rows_dev + cols_dev)
+    cols_g = jnp.where(
+        at < head,
+        at,
+        jnp.where(
+            at < head + rows_dev,
+            at + (link_idx * rows_dev - head),
+            at + (col_idx * cols_dev - head - rows_dev),
+        ),
+    )
 
     target_hot = targets[: head // tile_len + row_tiles, None] == jnp.arange(ntiles)[None, :]
     slack_some = jnp.sum(
@@ -194,8 +205,6 @@
     left = jnp.concatenate([chosen[:, mine], -rounded[:, mine]], 0)
     right = jnp.concatenate([chosen[:, head + rows_dev :], rounded[:, head + rows_dev :]], 0)
     matrix = contract_rows(left, right)
-    rows_g = cols_g[mine]
-    out_g = cols_g[head + rows_dev :]
     matrix = matrix + jnp.where(
         rows_g[:, None] == out_g[None, :], slack_rows[:, None], jnp.float32(0.0)
     )

time: 60.3 us -> 60.3 us (level)
  other arithmetic: 6.57 us -> 7.68 us
  local copies, waits for them, and re-layouts: 11.3 us -> 10.2 us
    broadcast_in_dim x2 -> x0, local copies, waits for them, and re-layouts: 1.12 us -> none  [the longest x1 0.59 us: local(): out_g[None, :] < head]
    add x1 -> x2, other arithmetic: 0.07 us -> 1.19 us  [the longest x1 0.6 us: local(): out_g = col_idx * cols_dev + jnp.arange(cols_dev)]
where the time goes in v5:
time: 60.3 us; the launch traced here: 59.8 us
  Pallas kernels  31.9 us (53%)
  local copies, waits for them, and re-layouts  10.2 us (17%)
  matrix products  9.73 us (16%)
  other arithmetic  7.68 us (13%)
    pallas_call x1, Pallas kernels, gather_blocks(): pl.pallas_call(functools.partial(gather_kernel, n), out_shape=jax.ShapeDt...  20.1 us
    pallas_call x2, Pallas kernels, inverse_factor(): pl.pallas_call(inverse_kernel, out_shape=jax.ShapeDtypeStruct((PANEL, PAN...  11.9 us
    dot_general x2, matrix products, local(): solved = jnp.dot(lower_inv, work, precision=lax.Precision.HIGHEST)  4.95 us
    unnamed x18, local copies, waits for them, and re-layouts  4.1 us
    dot_general x1, matrix products, local(): jnp.einsum('kjp,kju->kpu', onehot, all_vals, preferred_element_type=jnp.f...  2.68 us
    dot_general x3, matrix products, contract_rows(): lax.dot_general(left_side, right_side, (((0,), (0,)), ((), ())), preferre...  2.1 us
    select_n x1, local copies, waits for them, and re-layouts, local(): jnp.where(out_g[None, :] < head, padded, jnp.where(rows_g[:, None] < head...  1.81 us
    slice x2, local copies, waits for them, and re-layouts, local(): lower_inv = inverse_factor(work[:, first:first + PANEL])  1.27 us

profile of v5, /device:TPU:11, one launch (start us, length us, event | category | flops | bytes accessed | tf_op | source)
XLA Modules:
  0.0 59.8 jit_solution(5626321178858909774)
XLA Ops:
  0.0 0.7 %multiply_sqrt_fusion = f32[16]{0:T(128)S(1)} fusion(f32[16]{0:T(128)} %param.7), kind=kLoop, calls=%fused_computation.51 | loop fusion | flops 16 | bytes 128 | tf_op jit(solution)/shard_map/sqrt | solution.py:142
  1.2 0.6 iota_add_fusion.1
  1.9 0.8 %select_reduce_fusion.1 = s32[20]{0:T(128)S(1)} fusion(s32[32]{0:T(128)} %param.9, s32[20]{0:T(128)S(1)} %pad_add_fusion), kind=kLoop, calls=%fused_computation.36 | loop fusion | flops 1900 | bytes 288 | tf_op jit(solution)/shard_map/reduce_sum | solution.py:162
  2.8 0.8 %select_reduce_fusion = f32[4,128]{1,0:T(4,128)S(1)} fusion(f32[32,128]{1,0:T(8,128)} %bitcast.25, pred[4,32]{1,0:T(4,128)(4,1)S(1)} %iota_compare_fusion.6), kind=kLoop, calls=%fused_computation.34 | loop fusion | flops 32256 | bytes 18560 | tf_op jit(solution)/shard_map/reduce_sum | solution.py:180
  4.2 0.6 broadcast_compare_fusion
  4.8 0.7 %convert_element_type.27 = bf16[16,16]{1,0:T(8,128)(2,1)S(1)} convert(s32[16,16]{1,0:T(8,128)} %param.6) | non-fusion elementwise | flops 256 | bytes 1536 | tf_op jit(solution)/shard_map/convert_element_type | solution.py:145
  5.5 0.6 iota_add_fusion
  6.1 0.9 %multiply_convert_fusion = bf16[16,16,128]{2,1,0:T(8,128)(2,1)S(1)} fusion(bf16[16,16,128]{2,1,0:T(8,128)(2,1)} %param.5, f32[16]{0:T(128)S(1)} %multiply_sqrt_fusion), kind=kLoop, calls=%fused_computation.31 | loop fusion | flops 98304 | bytes 131136 | tf_op jit(solution)/shard_map/convert_element_type | solution.py:142
  7.0 0.6 %fusion.21.own_ref = bf16[272,128]{1,0:T(8,128)(2,1)} fusion(bf16[16,16]{1,0:T(8,128)(2,1)S(1)} %convert_element_type.27, bf16[256,128]{1,0:T(8,128)(2,1)S(1)} %bitcast.24), kind=kLoop, calls=%fused_computation.32 | loop fusion | flops 208896 | bytes 135680 | tf_op jit(solution)/shard_map/concatenate | solution.py:147
  8.0 20.1 %shard_map.55 = bf16[16,272,128]{2,1,0:T(8,128)(2,1)} custom-call(bf16[272,128]{1,0:T(8,128)(2,1)} %fusion.21.own_ref), custom_call_target="tpu_custom_call" | custom-call | tf_op jit(solution)/shard_map/pallas_call | solution.py:116
  28.1 0.9 %slice.58 = bf16[16,16,16]{2,1,0:T(8,128)(2,1)S(1)} slice(bf16[16,272,128]{2,1,0:T(8,128)(2,1)} %shard_map.55), slice={[0:16], [256:272], [0:16]} | slice | bytes 16384 | tf_op jit(solution)/shard_map/slice | solution.py:150
  29.3 2.7 %fusion.8 = bf16[256,20,128]{2,1,0:T(8,128)(2,1)S(1)} fusion(bf16[256,16,128]{2,1,0:T(8,128)(2,1)S(1)} %bitcast.23, s32[20]{0:T(128)S(1)} %select_reduce_fusion.1, s32[256,16]{1,0:T(8,128)S(1)} %bitcast_convert_fusion), kind=kOutput, calls=%fused_computation.18 | convolution fusion | flops 21708800 | bytes 2375760 | tf_op jit(solution)/shard_map/kjp,kju->kpu/dot_general | solution.py:164
  32.0 1.0 %copy.13 = bf16[256,20,128]{0,2,1:T(8,128)(2,1)S(1)} copy(bf16[256,20,128]{2,1,0:T(8,128)(2,1)S(1)} %fusion.8) | data formatting | bytes 2621440 | tf_op jit(solution)/shard_map/convert_element_type | solution.py:165
  33.3 1.4 %copy.20 = bf16[256,2048]{1,0:T(8,128)(2,1)} copy(bf16[256,2048]{0,1:T(8,128)(2,1)S(1)} %slice.87) | data formatting | bytes 2097152
  35.2 1.5 %copy-done = f32[256,2560]{1,0:T(8,128)} copy-done((f32[256,2560]{1,0:T(8,128)}, f32[256,2560]{1,0:T(8,128)S(1)}, u32[]{:S(2)}) %copy-start) | copy-done | bytes 2621464
  36.8 0.6 %slice.77.block_ref = f32[128,128]{1,0:T(8,128)} slice(f32[256,2560]{1,0:T(8,128)S(1)} %convolution_add_fusion), slice={[0:128], [0:128]} | slice | bytes 131072 | tf_op jit(solution)/shard_map/slice | solution.py:195
  37.4 5.9 %shard_map.56 = f32[128,128]{1,0:T(8,128)} custom-call(f32[128,128]{1,0:T(8,128)} %slice.77.block_ref), custom_call_target="tpu_custom_call" | custom-call | tf_op jit(solution)/shard_map/pallas_call | solution.py:65
  43.3 2.8 %fusion.24 = (bf16[128,2560]{1,0:T(8,128)(2,1)S(1)}, f32[128,2560]{1,0:T(8,128)S(1)}) fusion(f32[128,128]{1,0:T(8,128)} %shard_map.56, f32[256,2560]{1,0:T(8,128)} %copy-done, pred[256,2560]{1,0:T(32,128)(4,1)S(1)} %iota_compare_fusion.1), kind=kOutput, calls=%fused_computation.53 | convolution fusion | flops 503971840 | bytes 3670016 | tf_op jit(solution)/shard_map/dot_general | solution.py:196
  46.5 0.6 %slice.82.block_ref = f32[128,128]{1,0:T(8,128)} slice(f32[128,2560]{1,0:T(8,128)S(1)} %convolution_subtract_fusion), slice={[0:128], [128:256]} | slice | bytes 131072 | tf_op jit(solution)/shard_map/slice | solution.py:195
  47.1 5.9 %shard_map.57 = f32[128,128]{1,0:T(8,128)} custom-call(f32[128,128]{1,0:T(8,128)} %slice.82.block_ref), custom_call_target="tpu_custom_call" | custom-call | tf_op jit(solution)/shard_map/pallas_call | solution.py:65
  53.1 2.2 %convolution_select_fusion = f32[128,2560]{1,0:T(8,128)S(1)} fusion(f32[128,128]{1,0:T(8,128)} %shard_map.57, f32[128,2560]{1,0:T(8,128)S(1)} %convolution_subtract_fusion, pred[256,2560]{1,0:T(32,128)(4,1)S(1)} %iota_compare_fusion.1), kind=kOutput, calls=%fused_computation.1 | convolution fusion | flops 503644160 | bytes 3014656 | tf_op jit(solution)/shard_map/dot_general | solution.py:196
  55.7 1.0 %copy-done.2 = bf16[256,2048]{1,0:T(8,128)(2,1)S(1)} copy-done((bf16[256,2048]{1,0:T(8,128)(2,1)S(1)}, bf16[256,2048]{1,0:T(8,128)(2,1)}, u32[]{:S(2)}) %copy-start.2) | copy-done | bytes 1048600
  56.7 1.2 %fusion.1 = f32[256,2048]{0,1:T(8,128)S(1)} fusion(bf16[256,2048]{1,0:T(8,128)(2,1)S(1)} %slice.88, bf16[256,2048]{1,0:T(8,128)(2,1)S(1)} %copy-done.2, f32[256,256]{0,1:T(8,128)S(1)} %fusion.15, f32[256]{0:T(256)S(1)} %copy-done.5, s32[256]{0:T(256)S(1)} %copy-done.6, s32[2048]{0:T(1024)S(1)} %copy-done.3, pred[2048]{0:T(1024)(128)(4,1)S(1)} %copy-done.4, ...), kind=kOutput, calls=%fused_computation.9 | convolution fusion | flops 544210944 | bytes 4731136 | tf_op jit(solution)/shard_map/dot_general | solution.py:15
  58.0 1.8 %copy.17 = f32[256,2048]{1,0:T(8,128)} copy(f32[256,2048]{0,1:T(8,128)S(1)} %fusion.1) | data formatting | bytes 4194304 | tf_op jit(solution)/shard_map/jit(_where)/select_n | solution.py:212
  (35 shorter events, 3.4 us)
Async XLA Ops:
  28.1 1.3 %slice-start = ((bf16[16,272,128]{2,1,0:T(8,128)(2,1)}), bf16[16,256,128]{2,1,0:T(8,128)(2,1)S(1)}, s32[]{:S(2)}) async-start(bf16[16,272,128]{2,1,0:T(8,128)(2,1)} %shard_map.55), calls=%async_computation | async-start | bytes 2097152 | tf_op jit(solution)/shard_map/slice | solution.py:149
  35.2 1.5 %copy-start = (f32[256,2560]{1,0:T(8,128)}, f32[256,2560]{1,0:T(8,128)S(1)}, u32[]{:S(2)}) copy-start(f32[256,2560]{1,0:T(8,128)S(1)} %convolution_add_fusion) | copy-start | bytes 7864324
  43.3 2.8 %copy-start.1 = (f32[256,2560]{1,0:T(8,128)S(1)}, f32[256,2560]{1,0:T(8,128)}, u32[]{:S(2)}) copy-start(f32[256,2560]{1,0:T(8,128)} %copy-done) | copy-start | bytes 7864324
  55.5 1.2 %copy-start.2 = (bf16[256,2048]{1,0:T(8,128)(2,1)S(1)}, bf16[256,2048]{1,0:T(8,128)(2,1)}, u32[]{:S(2)}) copy-start(bf16[256,2048]{1,0:T(8,128)(2,1)} %copy.20) | copy-start | bytes 3145732
  55.5 1.2 %copy-start.3 = (s32[2048]{0:T(1024)S(1)}, s32[2048]{0:T(1024)}, u32[]{:S(2)}) copy-start(s32[2048]{0:T(1024)} %iota_add_fusion) | copy-start | bytes 24580
  55.5 1.2 %copy-start.4 = (pred[2048]{0:T(1024)(128)(4,1)S(1)}, pred[2048]{0:T(1024)(128)(4,1)}, u32[]{:S(2)}) copy-start(pred[2048]{0:T(1024)(128)(4,1)} %broadcast_compare_fusion) | copy-start | bytes 6148
  55.5 1.2 %copy-start.5 = (f32[256]{0:T(256)S(1)}, f32[256]{0:T(256)}, u32[]{:S(2)}) copy-start(f32[256]{0:T(256)} %get-tuple-element.5) | copy-start | bytes 3076
  55.5 1.2 %copy-start.6 = (s32[256]{0:T(256)S(1)}, s32[256]{0:T(256)}, u32[]{:S(2)}) copy-start(s32[256]{0:T(256)} %iota_add_fusion.1) | copy-start | bytes 3076
  55.5 1.2 %copy-start.7 = (pred[256]{0:T(512)(128)(4,1)S(1)}, pred[256]{0:T(512)(128)(4,1)}, u32[]{:S(2)}) copy-start(pred[256]{0:T(512)(128)(4,1)} %broadcast_compare_fusion.1) | copy-start | bytes 772
